TPU v7x, 32 devices: a whole 2x2x4 slice. The times are simulated.
32 devices in a mesh: groups: 2 (over x), tensor: 8 (over z, y), replica: 2 (over core).
Axes of the slice: x: 2, y: 2, z: 4, core: 2. Of those that a mesh axis runs over, the one named last changes fastest.
Arguments:
- fresh_activations: bfloat16 [64, 4, 5120], P(('groups', 'tensor', 'replica')), parts along dimension 0, may hold values from -6 to 6
- entry_norm_multiplier: float32 [10240], P('groups'), parts along dimension 0, may hold values from 0.1 to 1.9
- base_probe_projection: bfloat16 [10240, 8192], P('groups', 'tensor'), parts along dimension 0, may hold values from -0.078125 to 0.078125
- lookup_projection: bfloat16 [10240, 1024], P('groups', 'tensor'), parts along dimension 0, may hold values from -0.078125 to 0.078125
- contents_projection: bfloat16 [10240, 1024], P('groups', 'tensor'), parts along dimension 0, may hold values from -0.078125 to 0.078125
- base_result_projection: bfloat16 [16384, 5120], P(('groups', 'tensor')), parts along dimension 0, may hold values from -0.5 to 0.5
- probe_norm_multiplier: float32 [256], P('groups'), parts along dimension 0, may hold values from 0.1 to 1.9
- lookup_norm_multiplier: float32 [256], P('groups'), parts along dimension 0, may hold values from 0.1 to 1.9
- probe_narrowing_matrix: bfloat16 [10240, 64], P(('groups', 'tensor', 'replica')), parts along dimension 0, may hold values from -0.078125 to 0.078125
- probe_widening_matrix: bfloat16 [16384, 64], P(('groups', 'tensor', 'replica')), parts along dimension 0, may hold values from -0.375 to 0.375
- result_narrowing_matrix: bfloat16 [16384, 64], P(('groups', 'tensor', 'replica')), parts along dimension 0, may hold values from -0.0625 to 0.0625
- result_widening_matrix: bfloat16 [10240, 64], P(('groups', 'tensor', 'replica')), parts along dimension 0, may hold values from -2 to 2
- stored_rotated_lookups: bfloat16 [64, 8, 384, 128], P(('groups', 'tensor', 'replica')), parts along dimension 0, may hold values from -2.5 to 2.5
- stored_contents: bfloat16 [64, 8, 384, 128], P(('groups', 'tensor', 'replica')), parts along dimension 0, may hold values from -4 to 4
- stored_extent_per_sequence: int32 [64], P(('groups', 'tensor', 'replica')), parts along dimension 0, may hold values from 1 to 384, as said below
Outputs:
- attn_output: bfloat16 [64, 4, 5120], P(('groups', 'tensor', 'replica')), parts along dimension 0
There are 2 independent parts, one for each index of `groups`. A program takes and returns all parts, laid end to end along the dimension named above; each array names one. Nothing has to cross between parts.
Inputs may be any that keep to these rules, and one draw needn't show every extreme that they name: Row b's first stored_extent_per_sequence[b] slots are filled. In every draw the 2 rows of some aligned block of rows, which block drawn from the seed, all have length 384.
All inputs are finite; a program needn't handle non-finite values.
Results may differ from a plain program's by a relative error of at most 0.01.
Values may be sent and summed in bfloat16 or wider, within the bound.
A program may use at most 128 MiB of HBM per device.

v0:
```python
import jax
import jax.numpy as jnp
from jax import lax
from jax.sharding import PartitionSpec as P

QUESTION_GROUPS = 64
KEY_VALUE_HEADS = 8
ATTN_DEPTH = 128


delta_multiplier = 2.0
rope_base = 1000000.0


def rms_norm(value_rows, gain):
    return (
        value_rows
        * lax.rsqrt(jnp.mean(value_rows * value_rows, axis=-1, keepdims=True) + 1e-06)
        * gain
    )


def rotate(value_rows, positions):
    half = value_rows.shape[-1] // 2
    freqs = rope_base ** (-(jnp.arange(half, dtype=jnp.float32) * 2.0) / value_rows.shape[-1])
    angles = positions[..., None] * freqs
    cosine = jnp.cos(angles)
    sine = jnp.sin(angles)
    first = value_rows[..., :half]
    second = value_rows[..., half:]
    return jnp.concatenate(
        [first * cosine - second * sine, second * cosine + first * sine], axis=-1
    )


def attend(rot_query, rot_keys, new_values, stored_rotated_lookups, stored_contents, lengths):
    batch, token_steps, heads, width = rot_query.shape
    kv_heads = rot_keys.shape[2]
    group = heads // kv_heads
    scale = 1.0 / width**0.5
    query = rot_query.reshape(batch, token_steps, kv_heads, group, width)
    cached = (
        jnp.einsum(
            "bshgd,bhld->bhsgl", query, stored_rotated_lookups, preferred_element_type=jnp.float32
        )
        * scale
    )
    fresh = (
        jnp.einsum("bshgd,bthd->bhsgt", query, rot_keys, preferred_element_type=jnp.float32) * scale
    )
    slots = jnp.arange(stored_rotated_lookups.shape[2], dtype=jnp.int32)
    cache_mask = (slots[None, :] < lengths[:, None])[:, None, None, None, :]
    order = jnp.arange(token_steps, dtype=jnp.int32)
    fresh_mask = (order[None, :] <= order[:, None])[None, None, :, None, :]
    cached_exp = jnp.where(cache_mask, jnp.exp(cached), 0.0)
    fresh_exp = jnp.where(fresh_mask, jnp.exp(fresh), 0.0)
    denom = jnp.sum(cached_exp, axis=-1) + jnp.sum(fresh_exp, axis=-1)
    cached_w = (cached_exp / denom[..., None]).astype(jnp.bfloat16)
    fresh_w = (fresh_exp / denom[..., None]).astype(jnp.bfloat16)
    mixed = jnp.einsum(
        "bhsgl,bhld->bshgd", cached_w, stored_contents, preferred_element_type=jnp.float32
    )
    mixed = mixed + jnp.einsum(
        "bhsgt,bthd->bshgd", fresh_w, new_values, preferred_element_type=jnp.float32
    )
    return mixed.reshape(batch, token_steps, heads * width).astype(jnp.bfloat16)


def gather_pieces(wide, narrow):
    distribute_pieces = (
        lax.all_gather(wide[0], ("tensor", "replica"), axis=0, tiled=True),
        lax.all_gather(wide[1], ("tensor", "replica"), axis=0, tiled=True),
    )
    device_portion = (
        lax.all_gather(narrow[0], "replica", axis=0, tiled=True),
        lax.all_gather(narrow[1], "replica", axis=0, tiled=True),
    )
    return (distribute_pieces, device_portion)


def body(
    fresh_activations,
    entry_norm_multiplier,
    base_probe_projection,
    lookup_projection,
    contents_projection,
    base_result_projection,
    probe_norm_multiplier,
    lookup_norm_multiplier,
    probe_narrowing_matrix,
    probe_widening_matrix,
    result_narrowing_matrix,
    result_widening_matrix,
    stored_rotated_lookups,
    stored_contents,
    stored_extent_per_sequence,
):
    decode_row_count, token_steps, width = fresh_activations.shape
    normed = rms_norm(fresh_activations.astype(jnp.float32), entry_norm_multiplier).astype(
        jnp.bfloat16
    )
    distribute_pieces, device_portion = gather_pieces(
        (probe_narrowing_matrix, result_widening_matrix),
        (probe_widening_matrix, result_narrowing_matrix),
    )
    query_down_factor, output_up_factor = distribute_pieces
    query_up_factor, output_down_factor = device_portion
    merged_projection_back = (
        base_result_projection.astype(jnp.float32)
        + delta_multiplier
        * jnp.dot(output_down_factor, output_up_factor.T, preferred_element_type=jnp.float32)
    ).astype(jnp.bfloat16)
    merged_probe_projection = (
        base_probe_projection.astype(jnp.float32)
        + delta_multiplier
        * jnp.dot(query_down_factor, query_up_factor.T, preferred_element_type=jnp.float32)
    ).astype(jnp.bfloat16)
    packed = jnp.concatenate(
        [merged_probe_projection, lookup_projection, contents_projection], axis=1
    )
    query_feature_width = merged_probe_projection.shape[1]
    key_feature_width = lookup_projection.shape[1]
    packed_width = packed.shape[1]
    piece = lax.all_gather(normed, "tensor", axis=0, tiled=True)
    piece_rows = piece.shape[0]
    flattened_rows = piece.reshape(piece_rows * token_steps, width)
    projected = (
        jnp.dot(flattened_rows, packed, preferred_element_type=jnp.float32)
        .astype(jnp.bfloat16)
        .reshape(piece_rows, token_steps, packed_width)
    )
    received_shards = lax.all_to_all(projected, "tensor", split_axis=0, concat_axis=2, tiled=True)
    shards = lax.axis_size("tensor")
    received_shards = received_shards.reshape(decode_row_count, token_steps, shards, packed_width)
    query = received_shards[..., :query_feature_width].reshape(
        decode_row_count, token_steps, QUESTION_GROUPS, ATTN_DEPTH
    )
    key_rows = received_shards[
        ..., query_feature_width : query_feature_width + key_feature_width
    ].reshape(decode_row_count, token_steps, KEY_VALUE_HEADS, ATTN_DEPTH)
    value_rows = received_shards[..., query_feature_width + key_feature_width :].reshape(
        decode_row_count, token_steps, KEY_VALUE_HEADS, ATTN_DEPTH
    )
    positions = (
        stored_extent_per_sequence[:, None] + jnp.arange(token_steps, dtype=jnp.int32)[None, :]
    ).astype(jnp.float32)[:, :, None]
    rot_query = rotate(
        rms_norm(query.astype(jnp.float32), probe_norm_multiplier), positions
    ).astype(jnp.bfloat16)
    rot_keys = rotate(
        rms_norm(key_rows.astype(jnp.float32), lookup_norm_multiplier), positions
    ).astype(jnp.bfloat16)
    attended = attend(
        rot_query,
        rot_keys,
        value_rows,
        stored_rotated_lookups,
        stored_contents,
        stored_extent_per_sequence,
    )
    returned = lax.all_to_all(attended, "tensor", split_axis=2, concat_axis=0, tiled=True)
    amount = decode_row_count * lax.axis_size("tensor")
    flattened_rows = returned.reshape(amount * token_steps, returned.shape[2])
    total = lax.psum_scatter(
        jnp.dot(flattened_rows, merged_projection_back, preferred_element_type=jnp.float32).reshape(
            amount, token_steps, width
        ),
        "tensor",
        scatter_dimension=0,
        tiled=True,
    )
    return total.astype(jnp.bfloat16)


def solution(mesh):
    return jax.shard_map(
        body,
        mesh=mesh,
        in_specs=(
            P(("groups", "tensor", "replica"), None, None),
            P("groups"),
            P("groups", "tensor"),
            P("groups", "tensor"),
            P("groups", "tensor"),
            P(("groups", "tensor"), None),
            P("groups"),
            P("groups"),
            P(("groups", "tensor", "replica"), None),
            P(("groups", "tensor", "replica"), None),
            P(("groups", "tensor", "replica"), None),
            P(("groups", "tensor", "replica"), None),
            P(("groups", "tensor", "replica"), None, None, None),
            P(("groups", "tensor", "replica"), None, None, None),
            P(("groups", "tensor", "replica")),
        ),
        out_specs=P(("groups", "tensor", "replica"), None, None),
        check_vma=False,
    )
```

profile of v0, /device:TPU:0, one launch (start us, length us, event | category | flops | bytes accessed | tf_op | source)
XLA Modules:
  0.0 263.6 jit_solution(9170727634965497947)
XLA Ops:
  0.0 14.0 %copy.40 = bf16[5120,1024]{0,1:T(8,128)(2,1)} copy(bf16[5120,1024]{1,0:T(8,128)(2,1)} %param.17) | data formatting | bytes 20971520 | tf_op args[2]
  14.0 25.5 %all-gather = bf16[16,320,64]{1,2,0:T(8,128)(2,1)S(1)} all-gather(bf16[1,320,64]{1,2,0:T(8,128)(2,1)S(1)} %bitcast.77), channel_id=1, replica_groups=mesh['groups'=2,'tensor'=8,'replica'=2] {'tensor','replica'}, dimensions={0}, use_global_device_ids=true | all-gather | bytes 696320 | tf_op jit(solution)/shard_map/all_gather | solution.py:71
  39.4 0.5 copy.41
  39.9 0.6 reshape.125
  40.5 1.9 all_gather.17
  42.7 31.6 %all_gather.15 = bf16[16,4,5120]{2,1,0:T(4,128)(2,1)S(1)} all-gather(bf16[2,4,5120]{2,1,0:T(4,128)(2,1)S(1)} %fusion.38), channel_id=1, replica_groups=mesh['groups'=2,'tensor'=8,'replica'=2] {'tensor'}, dimensions={0}, use_global_device_ids=true | all-gather | bytes 737280 | tf_op jit(solution)/shard_map/all_gather | solution.py:124
  74.3 1.0 reshape.121
  75.4 2.4 copy.42
  77.8 2.5 copy.43
  80.3 5.6 %add_convert_fusion.1 = bf16[5120,1024]{0,1:T(8,128)(2,1)S(1)} fusion(bf16[5120,1024]{0,1:T(8,128)(2,1)} %copy.40, bf16[5120,64]{0,1:T(8,128)(2,1)S(1)} %reshape.125, bf16[1024,64]{0,1:T(8,128)(2,1)S(1)} %all_gather.17), kind=kOutput, calls=%fused_computation.1 | convolution fusion | flops 692060160 | bytes 21757952 | tf_op jit(solution)/shard_map/dot_general | solution.py:116
  86.0 9.1 %fusion.8 = bf16[64,1280]{1,0:T(8,128)(2,1)S(1)} fusion(bf16[64,5120]{1,0:T(8,128)(2,1)} %reshape.121, bf16[5120,128]{0,1:T(8,128)(2,1)} %copy.43, bf16[5120,128]{0,1:T(8,128)(2,1)} %copy.42, bf16[5120,1024]{0,1:T(8,128)(2,1)S(1)} %add_convert_fusion.1), kind=kOutput, calls=%fused_computation.10 | convolution fusion | flops 878264320 | bytes 13926400 | tf_op jit(solution)/shard_map/dot_general | solution.py:128
  95.1 0.7 reshape.122
  95.8 3.6 %all-to-all-start = ((bf16[16,4,1280]{2,1,0:T(4,128)(2,1)}), bf16[16,4,1280]{2,1,0:T(4,128)(2,1)S(1)}, u32[]{:S(2)}, u32[]{:S(2)}) async-start(bf16[16,4,1280]{2,1,0:T(4,128)(2,1)} %reshape.122), calls=%async_computation | async-start | bytes 327680 | tf_op jit(solution)/shard_map/all_to_all | solution.py:132
  99.7 7.0 %all-to-all-done = bf16[16,4,1280]{2,1,0:T(4,128)(2,1)S(1)} async-done(((bf16[16,4,1280]{2,1,0:T(4,128)(2,1)}), bf16[16,4,1280]{2,1,0:T(4,128)(2,1)S(1)}, u32[]{:S(2)}, u32[]{:S(2)}) %all-to-all-start) | async-done | bytes 163872 | tf_op jit(solution)/shard_map/all_to_all | solution.py:132
  107.6 0.8 fusion.51
  108.4 0.8 fusion.50
  109.3 0.2 convolution_bitcast_fusion
  109.5 1.9 fusion.30
  111.4 4.8 %copy.64 = bf16[2,4,8,8,128]{1,0,4,3,2:T(2,128)(2,1)} copy(bf16[2,4,8,8,128]{4,3,1,2,0:T(8,128)(2,1)S(1)} %fusion.30) | data formatting | bytes 262144 | tf_op jit(solution)/shard_map/convert_element_type | solution.py:66
  116.2 9.3 %reshape.134 = bf16[8,2,4096]{2,1,0:T(2,128)(2,1)} reshape(bf16[8192,2,4]{2,1,0:T(2,128)(2,1)} %bitcast.69) | data formatting | bytes 262144
  125.5 3.4 %all-to-all-start.1 = ((bf16[8,2,4096]{2,1,0:T(2,128)(2,1)}), bf16[8,2,4096]{2,1,0:T(2,128)(2,1)S(1)}, u32[]{:S(2)}, u32[]{:S(2)}) async-start(bf16[8,2,4096]{2,1,0:T(2,128)(2,1)} %reshape.134), calls=%async_computation.1 | async-start | bytes 262144 | tf_op jit(solution)/shard_map/all_to_all | solution.py:161
  128.9 23.9 %all-gather.1 = bf16[16,320,64]{1,2,0:T(8,128)(2,1)S(1)} all-gather(bf16[1,320,64]{1,2,0:T(8,128)(2,1)S(1)} %bitcast.78), channel_id=1, replica_groups=mesh['groups'=2,'tensor'=8,'replica'=2] {'tensor','replica'}, dimensions={0}, use_global_device_ids=true | all-gather | bytes 696320 | tf_op jit(solution)/shard_map/all_gather | solution.py:72
  152.8 0.5 copy.53
  153.3 0.6 reshape.127
  153.9 0.6 dynamic-slice
  155.2 2.1 all_gather.18
  157.3 10.0 %reshape.135 = bf16[8192,2,4]{2,1,0:T(2,128)(2,1)} reshape(bf16[8,2,4096]{2,1,0:T(2,128)(2,1)S(1)} %all-to-all-done.1) | data formatting | bytes 262144
  167.3 6.1 %copy.65 = bf16[2,4,8,1024]{3,2,1,0:T(8,128)(2,1)S(1)} copy(bf16[2,4,8,1024]{1,0,3,2:T(2,128)(2,1)} %bitcast.70) | data formatting | bytes 262144 | tf_op jit(solution)/shard_map/all_to_all | solution.py:161
  173.6 9.7 %fusion.6 = f32[16,4,5120]{2,0,1:T(8,128)} fusion(bf16[16,4,1024]{2,0,1:T(8,128)(2,1)S(1)} %dot_general.32, bf16[1024,5120]{1,0:T(8,128)(2,1)} %param.20, bf16[1024,64]{0,1:T(8,128)(2,1)S(1)} %all_gather.18, bf16[5120,64]{0,1:T(8,128)(2,1)S(1)} %reshape.127), kind=kOutput, calls=%fused_computation.8 | convolution fusion | flops 1363148800 | bytes 12713984 | tf_op jit(solution)/shard_map/dot_general | solution.py:165
  183.4 2.2 copy.54
  185.5 77.4 %all-reduce.2 = bf16[16,4,5120]{2,1,0:T(4,128)(2,1)S(1)} all-reduce(f32[16,4,5120]{2,1,0:T(4,128)S(1)} %copy.54), channel_id=2, replica_groups=mesh['groups'=2,'tensor'=8,'replica'=2] {'tensor'}, use_global_device_ids=true, to_apply=%region_5.6.clone | all-reduce | flops 327680 | bytes 1966080
  262.9 0.7 dynamic-slice_convert_fusion
  (47 shorter events, 1.7 us)
Async XLA Ops:
  0.0 108.4 %copy-start = (bf16[2,8,384,128]{3,2,1,0:T(8,128)(2,1)S(1)}, bf16[2,8,384,128]{3,2,1,0:T(8,128)(2,1)}, u32[]{:S(2)}) copy-start(bf16[2,8,384,128]{3,2,1,0:T(8,128)(2,1)} %param.27) | copy-start | bytes 4718596
  0.0 14.0 %copy-start.4 = (bf16[320,64]{0,1:T(8,128)(2,1)S(1)}, bf16[320,64]{0,1:T(8,128)(2,1)}, u32[]{:S(2)}) copy-start(bf16[320,64]{0,1:T(8,128)(2,1)} %param.23) | copy-start | bytes 122884
  0.0 40.5 %copy-start.2 = (bf16[512,64]{0,1:T(8,128)(2,1)S(1)}, bf16[512,64]{0,1:T(8,128)(2,1)}, u32[]{:S(2)}) copy-start(bf16[512,64]{0,1:T(8,128)(2,1)} %param.24) | copy-start | bytes 196612
  0.0 42.4 %copy-start.1 = (bf16[2,4,5120]{2,1,0:T(4,128)(2,1)S(1)}, bf16[2,4,5120]{2,1,0:T(4,128)(2,1)}, u32[]{:S(2)}) copy-start(bf16[2,4,5120]{2,1,0:T(4,128)(2,1)} %param.15) | copy-start | bytes 245764
  0.0 42.6 %copy-start.6 = (f32[5120]{0:T(1024)S(1)}, f32[5120]{0:T(1024)}, u32[]{:S(2)}) copy-start(f32[5120]{0:T(1024)} %param.16) | copy-start | bytes 61444
  85.9 13.5 %copy-start.9 = (s32[2]{0:T(128)S(1)}, s32[2]{0:T(128)}, u32[]{:S(2)}) copy-start(s32[2]{0:T(128)} %param.29) | copy-start | bytes 28
  85.9 21.1 %copy-start.7 = (f32[128]{0:T(128)S(1)}, f32[128]{0:T(128)}, u32[]{:S(2)}) copy-start(f32[128]{0:T(128)} %param.22) | copy-start | bytes 1540
  86.0 21.2 %copy-start.8 = (f32[128]{0:T(128)S(1)}, f32[128]{0:T(128)}, u32[]{:S(2)}) copy-start(f32[128]{0:T(128)} %param.21) | copy-start | bytes 1540
  95.1 33.8 %copy-start.5 = (bf16[320,64]{0,1:T(8,128)(2,1)S(1)}, bf16[320,64]{0,1:T(8,128)(2,1)}, u32[]{:S(2)}) copy-start(bf16[320,64]{0,1:T(8,128)(2,1)} %param.26) | copy-start | bytes 122884
  95.8 10.9 %all-to-all-start = ((bf16[16,4,1280]{2,1,0:T(4,128)(2,1)}), bf16[16,4,1280]{2,1,0:T(4,128)(2,1)S(1)}, u32[]{:S(2)}, u32[]{:S(2)}) async-start(bf16[16,4,1280]{2,1,0:T(4,128)(2,1)} %reshape.122), calls=%async_computation | async-start | bytes 327680 | tf_op jit(solution)/shard_map/all_to_all | solution.py:132
  107.6 46.3 %copy-start.10 = (u32[32]{0:T(128)S(1)}, u32[32]{0:T(128)}, u32[]{:S(2)}) copy-start(u32[32]{0:T(128)} %constant.31) | copy-start | bytes 388
  107.6 47.5 %copy-start.3 = (bf16[512,64]{0,1:T(8,128)(2,1)S(1)}, bf16[512,64]{0,1:T(8,128)(2,1)}, u32[]{:S(2)}) copy-start(bf16[512,64]{0,1:T(8,128)(2,1)} %param.25) | copy-start | bytes 196612
  125.5 31.8 %all-to-all-start.1 = ((bf16[8,2,4096]{2,1,0:T(2,128)(2,1)}), bf16[8,2,4096]{2,1,0:T(2,128)(2,1)S(1)}, u32[]{:S(2)}, u32[]{:S(2)}) async-start(bf16[8,2,4096]{2,1,0:T(2,128)(2,1)} %reshape.134), calls=%async_computation.1 | async-start | bytes 262144 | tf_op jit(solution)/shard_map/all_to_all | solution.py:161
where the time goes:
time: 265 us; the launch traced here: 264 us
  blocking collectives  162 us (61%)
  local copies, waits for them, and re-layouts  56.8 us (21%)
  matrix products  28.2 us (11%)
  waiting for transfers between devices  7.02 us (3%)
  starting transfers between devices  6.93 us (3%)
    unnamed x1, blocking collectives  77.4 us
    unnamed x30, local copies, waits for them, and re-layouts  40.1 us
    all_gather x1, blocking collectives, body(): piece = lax.all_gather(normed, 'tensor', axis=0, tiled=True)  31.6 us
    all_gather x1, blocking collectives, gather_pieces(): lax.all_gather(wide[0], ('tensor', 'replica'), axis=0, tiled=True)  25.5 us
    all_gather x1, blocking collectives, gather_pieces(): lax.all_gather(wide[1], ('tensor', 'replica'), axis=0, tiled=True)  23.9 us
    dot_general x1, matrix products, body(): jnp.dot(flattened_rows, merged_projection_back, preferred_element_type=jn...  9.74 us
    dot_general x1, matrix products, body(): jnp.dot(flattened_rows, packed, preferred_element_type=jnp.float32)  9.11 us
    all_to_all x1, waiting for transfers between devices, body(): lax.all_to_all(projected, 'tensor', split_axis=0, concat_axis=2, tiled=True)  7.02 us
  transfers between devices with their start and end apart: 2, of which 1 were waited for; matrix products, arithmetic and copies ran while one was open for 1% of the time, Pallas kernels for 0%

commit v1 on v0

--- a/solution.py
+++ b/solution.py
@@ -1,6 +1,11 @@
+import functools
+import math
+
 import jax
 import jax.numpy as jnp
 from jax import lax
+from jax.experimental import pallas as pl
+from jax.experimental.pallas import tpu as pltpu
 from jax.sharding import PartitionSpec as P
 
 QUESTION_GROUPS = 64
@@ -172,9 +177,466 @@
     return total.astype(jnp.bfloat16)
 
 
+BF16 = jnp.bfloat16
+F32 = jnp.float32
+MESH = pl.DeviceIdType.MESH
+
+
+def dot_nn(a, b):
+    return jnp.dot(a, b, preferred_element_type=F32)
+
+
+def dot_nt(a, b):
+    return lax.dot_general(a, b, (((1,), (1,)), ((), ())), preferred_element_type=F32)
+
+
+def fused_kernel(
+    n,
+    x_ref, gain_ref, wq_ref, wk_ref, wv_ref, wo_ref, qgain_ref, kgain_ref,
+    a_ref, b_ref, c_ref, d_ref, kc_ref, vc_ref, len_ref,
+    out_ref,
+    xs, w, wo, kbuf, vbuf, a2, b1, c2, d2, ts, us, acc, qs, qr, att_src, ar, abf, ps, rr, half_out, half_in,
+    loc, x_s, x_f, x_r, t_s, t_r, q_s, q_r, a_s, a_f, a_r, u_s, u_r, p_s, p_r, m_s, m_r,
+):
+    i = lax.axis_index("tensor")
+    r = lax.axis_index("replica")
+    o = 1 - r
+    me = 2 * i + r
+    width = x_ref.shape[1]
+    qcols = w.shape[1] - ATTN_DEPTH
+    ocols = wo.shape[1]
+    chunk = rr.shape[3]
+    chunks = ocols // chunk
+    slots_len = kc_ref.shape[2]
+
+    def peer(j, core):
+        return {"tensor": j, "replica": core}
+
+    def remote(src, dst, ssem, rsem, j, core):
+        return pltpu.make_async_remote_copy(
+            src_ref=src, dst_ref=dst, send_sem=ssem, recv_sem=rsem,
+            device_id=peer(j, core), device_id_type=MESH,
+        )
+
+    def ahead(d):
+        return lax.rem(i + d, n)
+
+    def behind(d):
+        return lax.rem(i + n - d, n)
+
+    barrier = pltpu.get_barrier_semaphore()
+
+    @pl.loop(1, 2 * n)
+    def _(d):
+        dev = lax.rem(me + d, 2 * n)
+        pl.semaphore_signal(barrier, inc=1, device_id=peer(dev // 2, lax.rem(dev, 2)), device_id_type=MESH)
+
+    cp_w = pltpu.make_async_copy(wq_ref.at[:, pl.ds(pl.multiple_of(r * qcols, 128), qcols)], w.at[:, pl.ds(0, qcols)], loc.at[0])
+    cp_w.start()
+    wkv_dst = w.at[:, pl.ds(qcols, ATTN_DEPTH)]
+    cp_k = pltpu.make_async_copy(wk_ref, wkv_dst, loc.at[1])
+    cp_v = pltpu.make_async_copy(wv_ref, wkv_dst, loc.at[1])
+
+    @pl.when(r == 0)
+    def _():
+        cp_k.start()
+
+    @pl.when(r == 1)
+    def _():
+        cp_v.start()
+
+    small = [
+        pltpu.make_async_copy(a_ref, a2.at[r], loc.at[2]),
+        pltpu.make_async_copy(b_ref, b1, loc.at[3]),
+        pltpu.make_async_copy(c_ref, c2.at[r], loc.at[4]),
+        pltpu.make_async_copy(d_ref, d2.at[r], loc.at[5]),
+    ]
+    caches = []
+    for b in range(2):
+        caches.append(pltpu.make_async_copy(kc_ref.at[b], kbuf.at[:, pl.ds(b * slots_len, slots_len), :], loc.at[6 + b]))
+        caches.append(pltpu.make_async_copy(vc_ref.at[b], vbuf.at[:, pl.ds(b * slots_len, slots_len), :], loc.at[8 + b]))
+    cp_wo = pltpu.make_async_copy(wo_ref.at[:, pl.ds(pl.multiple_of(r * ocols, 128), ocols)], wo, loc.at[10])
+    for cp in small + caches + [cp_wo]:
+        cp.start()
+
+    xf = x_ref[...].astype(F32)
+    inv = lax.rsqrt(jnp.mean(xf * xf, axis=-1, keepdims=True) + 1e-06)
+    xs[me] = (xf * inv * gain_ref[...]).astype(BF16)
+
+    pl.semaphore_wait(barrier, 2 * n - 1)
+
+    def x_direct(d):
+        return remote(xs.at[me], xs.at[me], x_s.at[d], x_r.at[me], ahead(d), r)
+
+    x_pair = remote(xs.at[me], xs.at[me], x_s.at[0], x_r.at[me], i, o)
+
+    @pl.loop(1, n)
+    def _(d):
+        x_direct(d).start()
+
+    x_pair.start()
+    lora_pair = [
+        remote(a_ref, a2.at[r], m_s.at[0], m_r.at[0], i, o),
+        remote(c_ref, c2.at[r], m_s.at[1], m_r.at[1], i, o),
+        remote(d_ref, d2.at[r], m_s.at[2], m_r.at[2], i, o),
+    ]
+    for cp in lora_pair:
+        cp.start()
+
+    row8 = lax.broadcasted_iota(jnp.int32, (8, ATTN_DEPTH), 0)
+    lane8 = lax.broadcasted_iota(jnp.int32, (8, ATTN_DEPTH), 1)
+    len0, len1 = len_ref[0], len_ref[1]
+    pos = (jnp.where(row8 < 4, len0, len1) + lax.rem(row8, 4)).astype(F32)
+    half_i = lax.rem(lane8, ATTN_DEPTH // 2).astype(F32)
+    freq = jnp.exp(half_i * (-2.0 / ATTN_DEPTH * math.log(rope_base)))
+    ang = pos * freq
+    cos8 = jnp.cos(ang)
+    sin8 = jnp.where(lane8 < ATTN_DEPTH // 2, -jnp.sin(ang), jnp.sin(ang))
+    kbuf[:, pl.ds(2 * slots_len, 128), :] = jnp.zeros((n, 128, ATTN_DEPTH), BF16)
+    vbuf[:, pl.ds(2 * slots_len, 128), :] = jnp.zeros((n, 128, ATTN_DEPTH), BF16)
+
+    def x_fwd(d, j):
+        s = 2 * j + r
+        return remote(xs.at[s], xs.at[s], x_f.at[d], x_r.at[s], i, o)
+
+    def x_arr(s):
+        return remote(xs.at[s], xs.at[s], x_s.at[0], x_r.at[s], i, o)
+
+    @pl.loop(1, n)
+    def _(d):
+        j = behind(d)
+        x_arr(2 * j + r).wait_recv()
+        x_fwd(d, j).start()
+
+    @pl.loop(0, n)
+    def _(d):
+        x_arr(2 * behind(d) + o).wait_recv()
+
+    def x_rows(k):
+        v = xs[:, :, pl.ds(pl.multiple_of(k * 640, 128), 640)]
+        return v.astype(F32).reshape(16 * 8, 640).astype(BF16)
+
+    def pack(t):
+        h = t.shape[0] // 2
+        return jnp.concatenate([t[:h], t[h:]], axis=1)
+
+    def unpack(t):
+        h = t.shape[1] // 2
+        return jnp.concatenate([t[:, :h], t[:, h:]], axis=0)
+
+    small[0].wait()
+    lora_pair[0].wait_recv()
+    t_mine = dot_nn(x_rows(i), a2[...].reshape(640, a2.shape[2]))
+    ts[i] = pack(t_mine).astype(BF16)
+
+    def t_copy(d):
+        return remote(ts.at[i], ts.at[i], t_s.at[d], t_r.at[i], ahead(d), r)
+
+    def t_arr(s):
+        return remote(ts.at[s], ts.at[s], t_s.at[0], t_r.at[s], i, o)
+
+    @pl.loop(1, n)
+    def _(d):
+        t_copy(d).start()
+
+    cp_w.wait()
+    cp_k.wait()
+    acc[...] = jnp.zeros_like(acc)
+
+    @pl.loop(0, width // 640)
+    def _(k):
+        acc[...] += dot_nn(x_rows(k), w[pl.ds(pl.multiple_of(k * 640, 128), 640), :])
+
+    @pl.loop(1, n)
+    def _(d):
+        t_arr(behind(d)).wait_recv()
+
+    small[1].wait()
+    t_all = unpack(jnp.sum(ts[...].astype(F32), axis=0)).astype(BF16)
+    acc[:, pl.ds(0, qcols)] += delta_multiplier * dot_nt(t_all, b1[...])
+    proj = acc[...].reshape(16, 8, w.shape[1]).astype(BF16)
+    qs[...] = proj
+
+    def q_copy(d):
+        dev = lax.rem(me + d, 2 * n)
+        return remote(qs.at[dev], qr.at[me], q_s.at[d], q_r.at[me], dev // 2, lax.rem(dev, 2))
+
+    def q_arr(s):
+        return remote(qr.at[s], qr.at[s], q_s.at[0], q_r.at[s], i, o)
+
+    @pl.loop(1, 2 * n)
+    def _(d):
+        q_copy(d).start()
+
+    qr[me] = qs[me]
+
+    @pl.loop(1, 2 * n)
+    def _(d):
+        q_arr(lax.rem(me + 2 * n - d, 2 * n)).wait_recv()
+
+    for cp in caches:
+        cp.wait()
+
+    heads = qcols // ATTN_DEPTH
+    rows = 2 * heads * 8
+    cos_q = jnp.concatenate([cos8] * (2 * heads), axis=0)
+    sin_q = jnp.concatenate([sin8] * (2 * heads), axis=0)
+    rb = lax.rem(lax.broadcasted_iota(jnp.int32, (rows, slots_len), 0), 8) // 4
+    cache_ok = lax.broadcasted_iota(jnp.int32, (rows, slots_len), 1) < jnp.where(rb == 0, len0, len1)
+    first_row = rb == 0
+    fr = lax.rem(lax.broadcasted_iota(jnp.int32, (rows, 128), 0), 8)
+    fc = lax.broadcasted_iota(jnp.int32, (rows, 128), 1)
+    fresh_ok = (fc // 4 == fr // 4) & (lax.rem(fc, 4) <= lax.rem(fr, 4))
+    scale = 1.0 / ATTN_DEPTH**0.5
+
+    def norm_rotate(v, gain, cosine, sine):
+        v = v * lax.rsqrt(jnp.mean(v * v, axis=-1, keepdims=True) + 1e-06) * gain
+        return (v * cosine + pltpu.roll(v, ATTN_DEPTH // 2, 1) * sine).astype(BF16)
+
+    def a_direct(j, d):
+        return remote(att_src.at[j], ar.at[me], a_s.at[d], a_r.at[me], j, r)
+
+    a_pair = remote(ar.at[me], ar.at[me], a_s.at[0], a_r.at[me], i, o)
+
+    def head_group(j):
+        q0 = qr[2 * j].astype(F32)
+        q1 = qr[2 * j + 1].astype(F32)
+        qh = jnp.concatenate(
+            [q[:, h * ATTN_DEPTH : (h + 1) * ATTN_DEPTH] for q in (q0, q1) for h in range(heads)], axis=0
+        )
+        q = norm_rotate(qh, qgain_ref[...], cos_q, sin_q)
+        kn = norm_rotate(q0[:, qcols:], kgain_ref[...], cos8, sin8).astype(F32)
+        pad = jnp.zeros((8, ATTN_DEPTH), F32)
+        kbuf[j, pl.ds(2 * slots_len, 16), :] = jnp.concatenate([kn, pad], axis=0).astype(BF16)
+        vbuf[j, pl.ds(2 * slots_len, 16), :] = jnp.concatenate([q1[:, qcols:], pad], axis=0).astype(BF16)
+        s = dot_nt(q, kbuf[j]) * scale
+        cached = jnp.where(first_row, s[:, :slots_len], s[:, slots_len : 2 * slots_len])
+        ec = jnp.where(cache_ok, jnp.exp(cached), 0.0)
+        ef = jnp.where(fresh_ok, jnp.exp(s[:, 2 * slots_len :]), 0.0)
+        denom = jnp.sum(ec, axis=-1, keepdims=True) + jnp.sum(ef, axis=-1, keepdims=True)
+        wc = ec / denom
+        wf = ef / denom
+        wgt = jnp.concatenate(
+            [jnp.where(first_row, wc, 0.0), jnp.where(first_row, 0.0, wc), wf], axis=1
+        ).astype(BF16)
+        o_ = dot_nn(wgt, vbuf[j])
+        return jnp.concatenate([o_[h * 8 : (h + 1) * 8] for h in range(2 * heads)], axis=1).astype(BF16)
+
+    @pl.loop(1, n)
+    def _(d):
+        j = ahead(d)
+        att_src[j] = head_group(j)
+        a_direct(j, d).start()
+
+    ar[me] = head_group(i)
+    a_pair.start()
+
+    def a_arr(s):
+        return remote(ar.at[s], ar.at[s], a_s.at[0], a_r.at[s], i, o)
+
+    def a_fwd(d, j):
+        s = 2 * j + r
+        return remote(ar.at[s], ar.at[s], a_f.at[d], a_r.at[s], i, o)
+
+    @pl.loop(1, n)
+    def _(d):
+        j = behind(d)
+        a_arr(2 * j + r).wait_recv()
+        a_fwd(d, j).start()
+
+    @pl.loop(0, n)
+    def _(d):
+        a_arr(2 * behind(d) + o).wait_recv()
+
+    abf[...] = ar[...].astype(F32).reshape(16 * 8, ar.shape[2]).astype(BF16)
+    small[2].wait()
+    lora_pair[1].wait_recv()
+    us[i] = pack(dot_nn(abf[...], c2[...].reshape(ar.shape[2], c2.shape[2]))).astype(BF16)
+
+    def u_copy(d):
+        return remote(us.at[i], us.at[i], u_s.at[d], u_r.at[i], ahead(d), r)
+
+    def u_arr(s):
+        return remote(us.at[s], us.at[s], u_s.at[0], u_r.at[s], i, o)
+
+    @pl.loop(1, n)
+    def _(d):
+        u_copy(d).start()
+
+    cp_wo.wait()
+    small[3].wait()
+    lora_pair[2].wait_recv()
+    own_chunk = lax.rem(i, chunks)
+
+    def p_copy(cc, d):
+        j = ahead(d)
+        return remote(ps.at[cc, j], rr.at[cc, i], p_s.at[cc, d], p_r.at[cc, i], j, r)
+
+    def p_arr(cc, s):
+        return remote(rr.at[cc, s], rr.at[cc, s], p_s.at[0, 0], p_r.at[cc, s], i, o)
+
+    def base(cc):
+        return dot_nn(abf[...], wo[:, pl.ds(pl.multiple_of(cc * chunk, 128), chunk)])
+
+    def ship(cc, part):
+        ps[cc] = part.astype(BF16).reshape(n, 16, chunk)
+
+        @pl.loop(1, n)
+        def _(d):
+            p_copy(cc, d).start()
+
+    @pl.loop(1, chunks)
+    def _(c):
+        cc = lax.rem(own_chunk + c, chunks)
+        ship(cc, base(cc))
+
+    last = base(own_chunk)
+
+    @pl.loop(1, n)
+    def _(d):
+        u_arr(behind(d)).wait_recv()
+
+    u_all = unpack(jnp.sum(us[...].astype(F32), axis=0)).astype(BF16)
+    mult = jnp.where(i // chunks == r, delta_multiplier, 0.0)
+    ship(own_chunk, last + mult * dot_nt(u_all, d2[...].reshape(640, d2.shape[2])))
+
+    @pl.loop(0, chunks)
+    def _(cc):
+        @pl.loop(1, n)
+        def _(d):
+            p_arr(cc, behind(d)).wait_recv()
+
+        rr[cc, i] = ps[cc, i]
+        total = jnp.sum(rr[cc].astype(F32), axis=0).reshape(2, 8, chunk)
+        mine = jnp.where(r == 0, total[0], total[1])
+        theirs = jnp.where(r == 0, total[1], total[0])
+        half_out[cc] = theirs
+        out_ref[:, pl.ds(pl.multiple_of(r * ocols + cc * chunk, 128), chunk)] = mine.astype(BF16)
+        remote(half_out.at[cc], half_in.at[cc], m_s.at[3 + cc], m_r.at[3 + cc], i, o).start()
+
+    @pl.loop(0, chunks)
+    def _(cc):
+        remote(half_out.at[cc], half_in.at[cc], m_s.at[3 + cc], m_r.at[3 + cc], i, o).wait()
+        out_ref[:, pl.ds(pl.multiple_of(o * ocols + cc * chunk, 128), chunk)] = half_in[cc].astype(BF16)
+
+    for cp in lora_pair:
+        cp.wait_send()
+    x_pair.wait_send()
+    a_pair.wait_send()
+
+    @pl.loop(1, n)
+    def _(d):
+        x_direct(d).wait_send()
+        x_fwd(d, behind(d)).wait_send()
+        t_copy(d).wait_send()
+        a_direct(ahead(d), d).wait_send()
+        a_fwd(d, behind(d)).wait_send()
+        u_copy(d).wait_send()
+        for cc in range(chunks):
+            p_copy(cc, d).wait_send()
+
+    @pl.loop(1, 2 * n)
+    def _(d):
+        q_copy(d).wait_send()
+
+
+def fused_body(
+    n,
+    fresh_activations,
+    entry_norm_multiplier,
+    base_probe_projection,
+    lookup_projection,
+    contents_projection,
+    base_result_projection,
+    probe_norm_multiplier,
+    lookup_norm_multiplier,
+    probe_narrowing_matrix,
+    probe_widening_matrix,
+    result_narrowing_matrix,
+    result_widening_matrix,
+    stored_rotated_lookups,
+    stored_contents,
+    stored_extent_per_sequence,
+):
+    rows_dev, steps, width = fresh_activations.shape
+    rows = rows_dev * steps
+    qcols = base_probe_projection.shape[1] // 2
+    ocols = width // 2
+    feats = base_result_projection.shape[0]
+    rank = probe_narrowing_matrix.shape[1]
+    part, up = probe_narrowing_matrix.shape[0], probe_widening_matrix.shape[0]
+    slots = stored_rotated_lookups.shape[2]
+    chunk = 2 * part
+    chunks = ocols // chunk
+    vmem = pl.BlockSpec(memory_space=pltpu.VMEM)
+    hbm = pl.BlockSpec(memory_space=pl.ANY)
+    smem = pl.BlockSpec(memory_space=pltpu.SMEM)
+    dma = pltpu.SemaphoreType.DMA
+    out = pl.pallas_call(
+        functools.partial(fused_kernel, n),
+        out_shape=jax.ShapeDtypeStruct((rows, width), BF16),
+        in_specs=[vmem, vmem, hbm, hbm, hbm, hbm, vmem, vmem, hbm, hbm, hbm, hbm, hbm, hbm, smem],
+        out_specs=vmem,
+        scratch_shapes=[
+            pltpu.VMEM((2 * n, rows, width), BF16),
+            pltpu.VMEM((width, qcols + ATTN_DEPTH), BF16),
+            pltpu.VMEM((feats, ocols), BF16),
+            pltpu.VMEM((n, 2 * slots + 128, ATTN_DEPTH), BF16),
+            pltpu.VMEM((n, 2 * slots + 128, ATTN_DEPTH), BF16),
+            pltpu.VMEM((2, part, rank), BF16),
+            pltpu.VMEM((up, rank), BF16),
+            pltpu.VMEM((2, up, rank), BF16),
+            pltpu.VMEM((2, part, rank), BF16),
+            pltpu.VMEM((n, n * rows, 2 * rank), BF16),
+            pltpu.VMEM((n, n * rows, 2 * rank), BF16),
+            pltpu.VMEM((2 * n * rows, qcols + ATTN_DEPTH), F32),
+            pltpu.VMEM((2 * n, rows, qcols + ATTN_DEPTH), BF16),
+            pltpu.VMEM((2 * n, rows, qcols + ATTN_DEPTH), BF16),
+            pltpu.VMEM((n, rows, feats), BF16),
+            pltpu.VMEM((2 * n, rows, feats), BF16),
+            pltpu.VMEM((2 * n * rows, feats), BF16),
+            pltpu.VMEM((chunks, n, 2 * rows, chunk), BF16),
+            pltpu.VMEM((chunks, n, 2 * rows, chunk), BF16),
+            pltpu.VMEM((chunks, rows, chunk), F32),
+            pltpu.VMEM((chunks, rows, chunk), F32),
+            dma((11,)),
+            dma((n,)), dma((n,)), dma((2 * n,)),
+            dma((n,)), dma((n,)),
+            dma((2 * n,)), dma((2 * n,)),
+            dma((n,)), dma((n,)), dma((2 * n,)),
+            dma((n,)), dma((n,)),
+            dma((chunks, n)), dma((chunks, n)),
+            dma((3 + chunks,)), dma((3 + chunks,)),
+        ],
+        compiler_params=pltpu.CompilerParams(
+            collective_id=0, has_side_effects=True, vmem_limit_bytes=56 * 1024 * 1024
+        ),
+        name="fused_attention_sync",
+    )(
+        fresh_activations.reshape(rows, width),
+        entry_norm_multiplier.reshape(1, width),
+        base_probe_projection,
+        lookup_projection,
+        contents_projection,
+        base_result_projection,
+        probe_norm_multiplier.reshape(1, ATTN_DEPTH),
+        lookup_norm_multiplier.reshape(1, ATTN_DEPTH),
+        probe_narrowing_matrix,
+        probe_widening_matrix,
+        result_narrowing_matrix,
+        result_widening_matrix,
+        stored_rotated_lookups,
+        stored_contents,
+        stored_extent_per_sequence,
+    )
+    return out.reshape(rows_dev, steps, width)
+
+
 def solution(mesh):
+    n = mesh.shape["tensor"]
+    fits = n == KEY_VALUE_HEADS and mesh.shape["replica"] == 2
     return jax.shard_map(
-        body,
+        functools.partial(fused_body, n) if fits else body,
         mesh=mesh,
         in_specs=(
             P(("groups", "tensor", "replica"), None, None),

time: 265 us -> 75.8 us (0.29)
  blocking collectives: 162 us -> 0 us
  Pallas kernels: 0 us -> 66 us
  local copies, waits for them, and re-layouts: 56.8 us -> 9.33 us
  matrix products: 28.2 us -> 0 us
  waiting for transfers between devices: 7.02 us -> 0 us
  starting transfers between devices: 6.93 us -> 0 us
    all_gather x5 -> x0, blocking collectives: 85 us -> none  [the longest x1 31.6 us: body(): piece = lax.all_gather(normed, 'tensor', axis=0, tiled=True)]
    unnamed x1 -> x0, blocking collectives: 77.4 us -> none
    pallas_call x0 -> x1, Pallas kernels: none -> 66 us  [fused_body(): pl.pallas_call(functools.partial(fused_kernel, n), out_shape=jax.ShapeDty...]
    unnamed x30 -> x4, local copies, waits for them, and re-layouts: 40.1 us -> 6.23 us
    dot_general x7 -> x0, matrix products: 28.2 us -> none  [the longest x1 9.74 us: body(): jnp.dot(flattened_rows, merged_projection_back, preferred_element_type=jn...]
    all_to_all x2 -> x0, waiting for transfers between devices: 7.02 us -> none  [the longest x1 7.02 us: body(): lax.all_to_all(projected, 'tensor', split_axis=0, concat_axis=2, tiled=True)]
    all_to_all x2 -> x0, starting transfers between devices: 6.93 us -> none  [the longest x1 3.56 us: body(): lax.all_to_all(projected, 'tensor', split_axis=0, concat_axis=2, tiled=True)]
    all_to_all x3 -> x0, local copies, waits for them, and re-layouts: 6.29 us -> none  [the longest x2 6.26 us: body(): lax.all_to_all(attended, 'tensor', split_axis=2, concat_axis=0, tiled=True)]
  transfers between devices with their start and end apart: 2 -> 0, of which waited for: 1 -> 0; matrix products, arithmetic and copies ran while one was open for 1% -> 0% of each run, Pallas kernels for 0% -> 0%
where the time goes in v1:
time: 75.8 us; the launch traced here: 75.3 us
  Pallas kernels  66 us (87%)
  local copies, waits for them, and re-layouts  9.33 us (12%)
    pallas_call x1, Pallas kernels, fused_body(): pl.pallas_call(functools.partial(fused_kernel, n), out_shape=jax.ShapeDty...  66 us
    unnamed x4, local copies, waits for them, and re-layouts  6.23 us
    reshape x1, local copies, waits for them, and re-layouts, fused_body(): return out.reshape(rows_dev, steps, width)  1.56 us
    reshape x1, local copies, waits for them, and re-layouts, fused_body(): fresh_activations.reshape(rows, width)  1.54 us

profile of v1, /device:TPU:0, one launch (start us, length us, event | category | flops | bytes accessed | tf_op | source)
XLA Modules:
  0.0 75.3 jit_solution(1476662215363079465)
XLA Ops:
  0.0 1.5 %reshape.15.x_ref = bf16[8,5120]{1,0:T(8,128)(2,1)} reshape(bf16[2,4,5120]{2,1,0:T(4,128)(2,1)} %param.15) | data formatting | bytes 163840 | tf_op jit(solution)/shard_map/reshape | solution.py:616
  1.5 1.5 %copy.16.a_ref = bf16[320,64]{1,0:T(8,128)(2,1)} copy(bf16[320,64]{0,1:T(8,128)(2,1)} %param.23) | data formatting | bytes 81920 | tf_op args[8]
  3.1 1.5 %copy.19.d_ref = bf16[320,64]{1,0:T(8,128)(2,1)} copy(bf16[320,64]{0,1:T(8,128)(2,1)} %param.26) | data formatting | bytes 81920 | tf_op args[11]
  4.6 1.6 %copy.17.b_ref = bf16[512,64]{1,0:T(8,128)(2,1)} copy(bf16[512,64]{0,1:T(8,128)(2,1)} %param.24) | data formatting | bytes 131072 | tf_op args[9]
  6.2 1.6 %copy.18.c_ref = bf16[512,64]{1,0:T(8,128)(2,1)} copy(bf16[512,64]{0,1:T(8,128)(2,1)} %param.25) | data formatting | bytes 131072 | tf_op args[10]
  7.8 66.0 %fused_attention_sync.1 = bf16[8,5120]{1,0:T(8,128)(2,1)} custom-call(bf16[8,5120]{1,0:T(8,128)(2,1)} %reshape.15.x_ref, f32[1,5120]{1,0:T(1,128)} %bitcast.3, bf16[5120,1024]{1,0:T(8,128)(2,1)} %wq_ref.1, bf16[5120,128]{1,0:T(8,128)(2,1)} %wk_ref.1, bf16[5120,128]{1,0:T(8,128)(2,1)} %wv_ref.1, bf16[1024,5120]{1,0:T(8,128)(2,1)} %wo_ref.1, ...), custom_call_target="tpu_custom_call" | custom-call | tf_op jit(solution)/shard_map/fused_attention_sync/pallas_call | solution.py:575
  73.8 1.6 %reshape.19 = bf16[2,4,5120]{2,1,0:T(4,128)(2,1)} reshape(bf16[8,5120]{1,0:T(8,128)(2,1)} %fused_attention_sync.1) | data formatting | bytes 163840 | tf_op jit(solution)/shard_map/reshape | solution.py:632

commit v2 on v1

--- a/solution.py
+++ b/solution.py
@@ -195,14 +195,14 @@
     x_ref, gain_ref, wq_ref, wk_ref, wv_ref, wo_ref, qgain_ref, kgain_ref,
     a_ref, b_ref, c_ref, d_ref, kc_ref, vc_ref, len_ref,
     out_ref,
-    xs, w, wo, kbuf, vbuf, a2, b1, c2, d2, ts, us, acc, qs, qr, att_src, ar, abf, ps, rr, half_out, half_in,
-    loc, x_s, x_f, x_r, t_s, t_r, q_s, q_r, a_s, a_f, a_r, u_s, u_r, p_s, p_r, m_s, m_r,
+    xs, w, wo, kbuf, vbuf, a2, b1, c2, d2, ts, us, acc, qs, qr, att_src, ar, abf, py, ry, own, ps, rr, half_out, half_in,
+    loc, x_s, x_f, x_r, t_s, t_r, q_s, q_r, a_s, a_f, a_r, u_s, u_r, y_s, y_r, p_s, p_r, m_s, m_r,
 ):
     i = lax.axis_index("tensor")
     r = lax.axis_index("replica")
     o = 1 - r
     me = 2 * i + r
-    width = x_ref.shape[1]
+    width = x_ref.shape[2]
     qcols = w.shape[1] - ATTN_DEPTH
     ocols = wo.shape[1]
     chunk = rr.shape[3]
@@ -223,6 +223,16 @@
 
     def behind(d):
         return lax.rem(i + n - d, n)
+
+    nz = n // 2
+    z, y = i // 2, lax.rem(i, 2)
+    side = i + 1 - 2 * y
+
+    def z_ahead(d):
+        return 2 * lax.rem(z + d, nz) + y
+
+    def z_behind(d):
+        return 2 * lax.rem(z + nz - d, nz) + y
 
     barrier = pltpu.get_barrier_semaphore()
 
@@ -259,21 +269,23 @@
     for cp in small + caches + [cp_wo]:
         cp.start()
 
-    xf = x_ref[...].astype(F32)
+    xf = jnp.concatenate([x_ref[0].astype(F32), x_ref[1].astype(F32)], axis=0)
     inv = lax.rsqrt(jnp.mean(xf * xf, axis=-1, keepdims=True) + 1e-06)
     xs[me] = (xf * inv * gain_ref[...]).astype(BF16)
 
     pl.semaphore_wait(barrier, 2 * n - 1)
 
     def x_direct(d):
-        return remote(xs.at[me], xs.at[me], x_s.at[d], x_r.at[me], ahead(d), r)
-
-    x_pair = remote(xs.at[me], xs.at[me], x_s.at[0], x_r.at[me], i, o)
-
-    @pl.loop(1, n)
+        return remote(xs.at[me], xs.at[me], x_s.at[d], x_r.at[me], z_ahead(d), r)
+
+    x_side = remote(xs.at[me], xs.at[me], x_s.at[0], x_r.at[me], side, r)
+    x_pair = remote(xs.at[me], xs.at[me], x_s.at[nz], x_r.at[me], i, o)
+
+    @pl.loop(1, nz)
     def _(d):
         x_direct(d).start()
 
+    x_side.start()
     x_pair.start()
     lora_pair = [
         remote(a_ref, a2.at[r], m_s.at[0], m_r.at[0], i, o),
@@ -295,18 +307,30 @@
     kbuf[:, pl.ds(2 * slots_len, 128), :] = jnp.zeros((n, 128, ATTN_DEPTH), BF16)
     vbuf[:, pl.ds(2 * slots_len, 128), :] = jnp.zeros((n, 128, ATTN_DEPTH), BF16)
 
-    def x_fwd(d, j):
-        s = 2 * j + r
-        return remote(xs.at[s], xs.at[s], x_f.at[d], x_r.at[s], i, o)
+    def x_fwd(k, s, j, core):
+        return remote(xs.at[s], xs.at[s], x_f.at[k], x_r.at[s], j, core)
+
+    def x_fwds(d):
+        s = 2 * z_behind(d) + r
+        return x_fwd(2 * d - 2, s, side, r), x_fwd(2 * d - 1, s, i, o)
+
+    def x_side_fwd(d):
+        s = 2 * (z_behind(d) + side - i) + r
+        return x_fwd(2 * nz - 2 + d, s, i, o)
 
     def x_arr(s):
         return remote(xs.at[s], xs.at[s], x_s.at[0], x_r.at[s], i, o)
 
-    @pl.loop(1, n)
-    def _(d):
-        j = behind(d)
-        x_arr(2 * j + r).wait_recv()
-        x_fwd(d, j).start()
+    @pl.loop(1, nz)
+    def _(d):
+        x_arr(2 * z_behind(d) + r).wait_recv()
+        for cp in x_fwds(d):
+            cp.start()
+
+    @pl.loop(0, nz)
+    def _(d):
+        x_arr(2 * (z_behind(d) + side - i) + r).wait_recv()
+        x_side_fwd(d).start()
 
     @pl.loop(0, n)
     def _(d):
@@ -326,7 +350,7 @@
 
     small[0].wait()
     lora_pair[0].wait_recv()
-    t_mine = dot_nn(x_rows(i), a2[...].reshape(640, a2.shape[2]))
+    t_mine = dot_nt(x_rows(i), jnp.concatenate([a2[0], a2[1]], axis=1))
     ts[i] = pack(t_mine).astype(BF16)
 
     def t_copy(d):
@@ -353,7 +377,7 @@
 
     small[1].wait()
     t_all = unpack(jnp.sum(ts[...].astype(F32), axis=0)).astype(BF16)
-    acc[:, pl.ds(0, qcols)] += delta_multiplier * dot_nt(t_all, b1[...])
+    acc[:, pl.ds(0, qcols)] += delta_multiplier * dot_nn(t_all, b1[...])
     proj = acc[...].reshape(16, 8, w.shape[1]).astype(BF16)
     qs[...] = proj
 
@@ -451,7 +475,7 @@
     abf[...] = ar[...].astype(F32).reshape(16 * 8, ar.shape[2]).astype(BF16)
     small[2].wait()
     lora_pair[1].wait_recv()
-    us[i] = pack(dot_nn(abf[...], c2[...].reshape(ar.shape[2], c2.shape[2]))).astype(BF16)
+    us[i] = pack(dot_nt(abf[...], jnp.concatenate([c2[0], c2[1]], axis=1))).astype(BF16)
 
     def u_copy(d):
         return remote(us.at[i], us.at[i], u_s.at[d], u_r.at[i], ahead(d), r)
@@ -468,9 +492,15 @@
     lora_pair[2].wait_recv()
     own_chunk = lax.rem(i, chunks)
 
+    def order(k):
+        return lax.rem(2 * (i // 2) + 2 + k, chunks)
+
+    def y_copy(cc):
+        return remote(py.at[cc], ry.at[cc], y_s.at[cc], y_r.at[cc], side, r)
+
     def p_copy(cc, d):
-        j = ahead(d)
-        return remote(ps.at[cc, j], rr.at[cc, i], p_s.at[cc, d], p_r.at[cc, i], j, r)
+        j = z_ahead(d)
+        return remote(ps.at[cc, j // 2], rr.at[cc, z], p_s.at[cc, d], p_r.at[cc, z], j, r)
 
     def p_arr(cc, s):
         return remote(rr.at[cc, s], rr.at[cc, s], p_s.at[0, 0], p_r.at[cc, s], i, o)
@@ -479,35 +509,47 @@
         return dot_nn(abf[...], wo[:, pl.ds(pl.multiple_of(cc * chunk, 128), chunk)])
 
     def ship(cc, part):
-        ps[cc] = part.astype(BF16).reshape(n, 16, chunk)
-
-        @pl.loop(1, n)
+        v = part.reshape(nz, 2, 16, chunk)
+        own[cc] = jnp.where(y == 0, v[:, 0], v[:, 1])
+        py[cc] = jnp.where(y == 0, v[:, 1], v[:, 0]).astype(BF16)
+        y_copy(cc).start()
+
+    def merge(cc):
+        y_copy(cc).wait_recv()
+        v = own[cc] + ry[cc].astype(F32)
+        own[cc] = v
+        ps[cc] = v.astype(BF16)
+
+        @pl.loop(1, nz)
         def _(d):
             p_copy(cc, d).start()
 
-    @pl.loop(1, chunks)
-    def _(c):
-        cc = lax.rem(own_chunk + c, chunks)
-        ship(cc, base(cc))
-
-    last = base(own_chunk)
+    ship(order(0), base(order(0)))
+    ship(order(1), base(order(1)))
+    merge(order(0))
 
     @pl.loop(1, n)
     def _(d):
         u_arr(behind(d)).wait_recv()
 
     u_all = unpack(jnp.sum(us[...].astype(F32), axis=0)).astype(BF16)
-    mult = jnp.where(i // chunks == r, delta_multiplier, 0.0)
-    ship(own_chunk, last + mult * dot_nt(u_all, d2[...].reshape(640, d2.shape[2])))
+    low = dot_nn(u_all, jnp.concatenate([d2[0], d2[1]], axis=1))
+    for k in (2, 3):
+        cc = order(k)
+        mult = jnp.where((cc == own_chunk) & (i // chunks == r), delta_multiplier, 0.0)
+        ship(cc, base(cc) + mult * low)
+        merge(order(k - 1))
+    merge(order(3))
 
     @pl.loop(0, chunks)
-    def _(cc):
-        @pl.loop(1, n)
-        def _(d):
-            p_arr(cc, behind(d)).wait_recv()
-
-        rr[cc, i] = ps[cc, i]
-        total = jnp.sum(rr[cc].astype(F32), axis=0).reshape(2, 8, chunk)
+    def _(k):
+        cc = order(k)
+        total = own[cc, z]
+        for d in range(1, nz):
+            s = z_behind(d) // 2
+            p_arr(cc, s).wait_recv()
+            total = total + rr[cc, s].astype(F32)
+        total = total.reshape(2, 8, chunk)
         mine = jnp.where(r == 0, total[0], total[1])
         theirs = jnp.where(r == 0, total[1], total[0])
         half_out[cc] = theirs
@@ -515,25 +557,36 @@
         remote(half_out.at[cc], half_in.at[cc], m_s.at[3 + cc], m_r.at[3 + cc], i, o).start()
 
     @pl.loop(0, chunks)
-    def _(cc):
+    def _(k):
+        cc = order(k)
         remote(half_out.at[cc], half_in.at[cc], m_s.at[3 + cc], m_r.at[3 + cc], i, o).wait()
         out_ref[:, pl.ds(pl.multiple_of(o * ocols + cc * chunk, 128), chunk)] = half_in[cc].astype(BF16)
 
     for cp in lora_pair:
         cp.wait_send()
     x_pair.wait_send()
+    x_side.wait_send()
     a_pair.wait_send()
 
+    @pl.loop(1, nz)
+    def _(d):
+        x_direct(d).wait_send()
+        for cp in x_fwds(d):
+            cp.wait_send()
+        for cc in range(chunks):
+            p_copy(cc, d).wait_send()
+
+    @pl.loop(0, nz)
+    def _(d):
+        x_side_fwd(d).wait_send()
+        y_copy(d).wait_send()
+
     @pl.loop(1, n)
     def _(d):
-        x_direct(d).wait_send()
-        x_fwd(d, behind(d)).wait_send()
         t_copy(d).wait_send()
         a_direct(ahead(d), d).wait_send()
         a_fwd(d, behind(d)).wait_send()
         u_copy(d).wait_send()
-        for cc in range(chunks):
-            p_copy(cc, d).wait_send()
 
     @pl.loop(1, 2 * n)
     def _(d):
@@ -583,10 +636,10 @@
             pltpu.VMEM((feats, ocols), BF16),
             pltpu.VMEM((n, 2 * slots + 128, ATTN_DEPTH), BF16),
             pltpu.VMEM((n, 2 * slots + 128, ATTN_DEPTH), BF16),
-            pltpu.VMEM((2, part, rank), BF16),
-            pltpu.VMEM((up, rank), BF16),
-            pltpu.VMEM((2, up, rank), BF16),
-            pltpu.VMEM((2, part, rank), BF16),
+            pltpu.VMEM((2, rank, part), BF16),
+            pltpu.VMEM((rank, up), BF16),
+            pltpu.VMEM((2, rank, up), BF16),
+            pltpu.VMEM((2, rank, part), BF16),
             pltpu.VMEM((n, n * rows, 2 * rank), BF16),
             pltpu.VMEM((n, n * rows, 2 * rank), BF16),
             pltpu.VMEM((2 * n * rows, qcols + ATTN_DEPTH), F32),
@@ -595,17 +648,17 @@
             pltpu.VMEM((n, rows, feats), BF16),
             pltpu.VMEM((2 * n, rows, feats), BF16),
             pltpu.VMEM((2 * n * rows, feats), BF16),
-            pltpu.VMEM((chunks, n, 2 * rows, chunk), BF16),
-            pltpu.VMEM((chunks, n, 2 * rows, chunk), BF16),
+            *[pltpu.VMEM((chunks, n // 2, 2 * rows, chunk), dt) for dt in (BF16, BF16, F32, BF16, BF16)],
             pltpu.VMEM((chunks, rows, chunk), F32),
             pltpu.VMEM((chunks, rows, chunk), F32),
             dma((11,)),
-            dma((n,)), dma((n,)), dma((2 * n,)),
+            dma((n,)), dma((2 * n,)), dma((2 * n,)),
             dma((n,)), dma((n,)),
             dma((2 * n,)), dma((2 * n,)),
             dma((n,)), dma((n,)), dma((2 * n,)),
             dma((n,)), dma((n,)),
-            dma((chunks, n)), dma((chunks, n)),
+            dma((chunks,)), dma((chunks,)),
+            dma((chunks, n // 2)), dma((chunks, n // 2)),
             dma((3 + chunks,)), dma((3 + chunks,)),
         ],
         compiler_params=pltpu.CompilerParams(
@@ -613,7 +666,7 @@
         ),
         name="fused_attention_sync",
     )(
-        fresh_activations.reshape(rows, width),
+        fresh_activations,
         entry_norm_multiplier.reshape(1, width),
         base_probe_projection,
         lookup_projection,
@@ -621,10 +674,10 @@
         base_result_projection,
         probe_norm_multiplier.reshape(1, ATTN_DEPTH),
         lookup_norm_multiplier.reshape(1, ATTN_DEPTH),
-        probe_narrowing_matrix,
-        probe_widening_matrix,
-        result_narrowing_matrix,
-        result_widening_matrix,
+        probe_narrowing_matrix.T,
+        probe_widening_matrix.T,
+        result_narrowing_matrix.T,
+        result_widening_matrix.T,
         stored_rotated_lookups,
         stored_contents,
         stored_extent_per_sequence,

time: 75.8 us -> 61.3 us (0.81)
  local copies, waits for them, and re-layouts: 9.33 us -> 1.56 us
  Pallas kernels: 66 us -> 59.5 us
    pallas_call x1, Pallas kernels: 66 us -> 59.5 us  [fused_body(): pl.pallas_call(functools.partial(fused_kernel, n), out_shape=jax.ShapeDty...]
    unnamed x4 -> x0, local copies, waits for them, and re-layouts: 6.23 us -> none
    reshape x1 -> x0, local copies, waits for them, and re-layouts: 1.54 us -> none  [fused_body(): fresh_activations.reshape(rows, width)]
where the time goes in v2:
time: 61.3 us; the launch traced here: 61.1 us
  Pallas kernels  59.5 us (97%)
  local copies, waits for them, and re-layouts  1.56 us (3%)
    pallas_call x1, Pallas kernels, fused_body(): pl.pallas_call(functools.partial(fused_kernel, n), out_shape=jax.ShapeDty...  59.5 us
    reshape x1, local copies, waits for them, and re-layouts, fused_body(): return out.reshape(rows_dev, steps, width)  1.56 us

profile of v2, /device:TPU:0, one launch (start us, length us, event | category | flops | bytes accessed | tf_op | source)
XLA Modules:
  0.0 61.1 jit_solution(11117575089469264160)
XLA Ops:
  0.0 59.5 %fused_attention_sync.1 = bf16[8,5120]{1,0:T(8,128)(2,1)} custom-call(bf16[2,4,5120]{2,1,0:T(4,128)(2,1)} %x_ref.1, f32[1,5120]{1,0:T(1,128)} %bitcast.11, bf16[5120,1024]{1,0:T(8,128)(2,1)} %wq_ref.1, bf16[5120,128]{1,0:T(8,128)(2,1)} %wk_ref.1, bf16[5120,128]{1,0:T(8,128)(2,1)} %wv_ref.1, bf16[1024,5120]{1,0:T(8,128)(2,1)} %wo_ref.1, f32[1,128]{1,0:T(1,128)} %bitcast.12, ...), custom_call_target="tpu_custom_call" | custom-call | tf_op jit(solution)/shard_map/fused_attention_sync/pallas_call | solution.py:628
  59.5 1.6 %reshape.15 = bf16[2,4,5120]{2,1,0:T(4,128)(2,1)} reshape(bf16[8,5120]{1,0:T(8,128)(2,1)} %fused_attention_sync.1) | data formatting | bytes 163840 | tf_op jit(solution)/shard_map/reshape | solution.py:685
